TPU v7x, 256 devices: a whole 4x4x8 slice. The times are simulated.
256 devices in a mesh: tok: 64 (over x, z, core), hid: 4 (over y).
Axes of the slice: x: 4, y: 4, z: 8, core: 2. Of those that a mesh axis runs over, the one named last changes fastest.
Arguments:
- activations: bfloat16 [131072, 8192], P('tok', 'hid'), may hold values from -6 to 6
- sketch: bfloat16 [8192, 320], P('hid'), may hold values from -0.0625 to 0.0625
Outputs:
- basis: float32 [131072, 320], P('tok')
- projected: float32 [8192, 320], P(('hid', 'tok'))
All inputs are finite; a program needn't handle non-finite values.
Results may differ from a plain program's by a relative error of at most 0.00069.
Values sent between devices are 32-bit elements; how exact they have to be, the bound alone decides.
A program may use at most 128 MiB of HBM per device.

v0:
```python
import jax
import jax.numpy as jnp
from jax import lax
from jax.sharding import PartitionSpec as P


def local(activations, sketch):
    partial_rows = jnp.dot(activations, sketch, preferred_element_type=jnp.float32)
    sampled = lax.psum(partial_rows, "hid")
    local_gram = jnp.dot(
        sampled.T, sampled, precision=lax.Precision.HIGHEST, preferred_element_type=jnp.float32
    )
    gram = lax.psum(local_gram, "tok")
    lower = jnp.linalg.cholesky(gram)
    basis = lax.linalg.triangular_solve(
        lower, sampled, left_side=False, lower=True, transpose_a=True
    )
    basis_bf = basis.astype(jnp.bfloat16)
    width = activations.shape[1] // lax.axis_size("tok")
    terms = lax.dot_general(
        activations, basis_bf, (((0,), (0,)), ((), ())), preferred_element_type=jnp.float32
    )
    summed = lax.psum(terms, "tok")
    projected = lax.dynamic_slice_in_dim(summed, lax.axis_index("tok") * width, width, 0)
    return (basis, projected)


def solution(mesh):
    in_specs = (P("tok", "hid"), P("hid", None))
    out_specs = (P("tok", None), P(("hid", "tok"), None))
    return jax.shard_map(local, mesh=mesh, in_specs=in_specs, out_specs=out_specs, check_vma=False)
```

profile of v0, /device:TPU:1, one launch (start us, length us, event | category | flops | bytes accessed | tf_op | source)
XLA Modules:
  0.0 581.2 jit_solution(3325697537734656014)
XLA Ops:
  7.2 0.0 copy-start
  7.2 0.0 all-reduce.7.cloned.1.call-start
  7.2 1.3 copy-done
  8.5 7.8 %fusion.21 = f32[2048,320]{0,1:T(8,128)} fusion(bf16[2048,2048]{1,0:T(8,128)(2,1)} %param.2, bf16[2048,320]{0,1:T(8,128)(2,1)S(1)} %copy-done), kind=kOutput, calls=%fused_computation.57 | convolution fusion | flops 2684354560 | bytes 12320768 | tf_op jit(solution)/shard_map/dot_general | solution.py:8
  16.3 0.0 all-reduce.7.cloned.1.call-update
  16.3 0.0 all-reduce.9.cloned.1.call-start
  16.4 76.3 %all-reduce.7.cloned.1.call-done = f32[2048,320]{0,1:T(8,128)} async-done(((f32[2048,320]{0,1:T(8,128)}), f32[2048,320]{0,1:T(8,128)}) %all-reduce.7.cloned.1.call-update) | async-done | bytes 2621456 | tf_op jit(solution)/shard_map/psum | solution.py:9
  92.6 7.5 %fusion.22 = f32[320,320]{0,1:T(8,128)} fusion(f32[2048,320]{0,1:T(8,128)} %all-reduce.7.cloned.1.call-done), kind=kOutput, calls=%fused_computation.58 | convolution fusion | flops 2516582400 | bytes 3031040 | tf_op jit(solution)/shard_map/dot_general | solution.py:10
  100.2 0.0 all-reduce.9.cloned.1.call-update
  100.2 0.2 all-reduce.11.cloned.1.call-start
  100.5 179.0 %all-reduce.9.cloned.1.call-done = f32[320,320]{0,1:T(8,128)} async-done(((f32[320,320]{0,1:T(8,128)}), f32[320,320]{0,1:T(8,128)}) %all-reduce.9.cloned.1.call-update) | async-done | bytes 409616 | tf_op jit(solution)/shard_map/psum | solution.py:13
  279.4 1.2 copy.5
  280.7 1.1 fusion.6
  281.8 11.7 %cholesky.78 = f32[128,128]{1,0:T(8,128)S(1)} custom-call(f32[128,128]{1,0:T(8,128)S(1)} %cholesky.198), custom_call_target="Cholesky" | custom-call | tf_op jit(solution)/shard_map/jit(cholesky)/cholesky | solution.py:14
  293.5 9.8 %custom-call.22 = f32[1,128,128]{1,2,0:T(8,128)S(1)} custom-call(f32[1,128,128]{2,1,0:T(8,128)S(1)} %get-tuple-element.26), custom_call_target="InvertDiagBlocksLowerTriangular" | custom-call | tf_op jit(solution)/shard_map/jit(cholesky)/cholesky | solution.py:14
  303.4 0.2 constant_dynamic-update-slice_fusion.2
  303.6 0.3 convolution_subtract_fusion.2
  303.9 11.7 %cholesky.164 = f32[128,128]{1,0:T(8,128)S(1)} custom-call(f32[128,128]{1,0:T(8,128)S(1)} %cholesky.202), custom_call_target="Cholesky" | custom-call | tf_op jit(solution)/shard_map/jit(cholesky)/cholesky | solution.py:14
  315.7 10.0 %custom-call.23 = f32[1,128,128]{1,2,0:T(8,128)S(1)} custom-call(f32[1,128,128]{2,1,0:T(8,128)S(1)} %get-tuple-element.23), custom_call_target="InvertDiagBlocksLowerTriangular" | custom-call | tf_op jit(solution)/shard_map/jit(cholesky)/cholesky | solution.py:14
  325.7 0.2 convolution_dynamic-update-slice_fusion
  325.9 0.2 convolution_subtract_fusion.3
  326.1 5.8 %cholesky.186 = f32[64,64]{1,0:T(8,128)S(1)} custom-call(f32[64,64]{1,0:T(8,128)S(1)} %convolution_subtract_fusion.3), custom_call_target="Cholesky" | custom-call | tf_op jit(solution)/shard_map/jit(cholesky)/cholesky | solution.py:14
  332.0 0.6 compare_reduce_fusion
  332.6 0.6 compare_reduce_fusion.1
  335.3 0.1 triangular_solve.94
  335.3 4.0 while.1
  335.3 0.6 fusion.33
  335.9 1.4 bitcast_dynamic-update-slice_fusion.2
  337.3 0.6 fusion.33
  337.9 1.4 bitcast_dynamic-update-slice_fusion.2
  339.3 0.1 fusion.12
  339.4 29.5 %custom-call.24 = f32[3,128,128]{1,2,0:T(8,128)S(1)} custom-call(f32[3,128,128]{2,1,0:T(8,128)S(1)} %pad_maximum_fusion.1), custom_call_target="InvertDiagBlocksLowerTriangular" | custom-call | tf_op jit(solution)/shard_map/triangular_solve | solution.py:15
  368.9 0.0 slice-start
  368.9 2.5 fusion.4
  371.4 2.3 convolution_subtract_fusion
  373.7 1.1 fusion.10
  374.8 0.0 slice-start.1
  374.8 2.7 convolution_subtract_fusion.1
  377.5 0.6 fusion.17
  378.1 0.3 pad_maximum_fusion
  378.4 0.0 copy-start.1
  378.4 1.5 copy-done.1
  379.9 0.0 slice-done
  379.9 0.0 slice-done.1
  379.9 4.4 convolution_bitcast_fusion
  384.3 0.0 all-reduce.11.cloned.1.call-update
  384.4 188.5 %all-reduce.11.cloned.1.call-done = f32[2048,320]{0,1:T(8,128)} async-done(((f32[2048,320]{0,1:T(8,128)}), f32[2048,320]{0,1:T(8,128)}) %all-reduce.11.cloned.1.call-update) | async-done | bytes 2621456 | tf_op jit(solution)/shard_map/psum | solution.py:23
  572.9 1.0 constant_dynamic-slice_fusion.1
  573.9 0.7 copy.6
  (16 shorter events, 0.3 us)
Async XLA Ops:
  7.2 1.3 copy-start
  7.2 85.5 %all-reduce.7.cloned.1.call-start = ((), (), s32[]{:S(2)}) async-start(), calls=%async_computation | async-start | bytes 5242880 | tf_op jit(solution)/shard_map/psum | solution.py:9
  16.3 263.2 %all-reduce.9.cloned.1.call-start = ((), (), s32[]{:S(2)}) async-start(), calls=%async_computation.1 | async-start | bytes 983040 | tf_op jit(solution)/shard_map/psum | solution.py:13
  100.2 472.7 %all-reduce.11.cloned.1.call-start = ((), (), s32[]{:S(2)}) async-start(), calls=%async_computation.2 | async-start | bytes 5242880 | tf_op jit(solution)/shard_map/psum | solution.py:23
  368.9 11.0 %slice-start = ((s8[8388608]{0:T(1024)(128)(4,1)}), s8[4194304]{0:T(1024)(128)(4,1)S(1)}, s32[]{:S(2)}) async-start(s8[8388608]{0:T(1024)(128)(4,1)} %bitcast.48), calls=%async_computation.3 | async-start | bytes 8388608
  374.8 5.1 slice-start.1
  378.4 1.5 copy-start.1
Sparse Core Ops, SparseCore 0:
  16.4 76.1 all-reduce.6
  100.3 179.0 all-reduce.8
  384.5 188.3 all-reduce.10
where the time goes:
time: 583 us; the launch traced here: 581 us
  waiting for transfers between devices  444 us (76%)
  other arithmetic  81.5 us (14%)
  matrix products  29.8 us (5%)
  between operations  15.9 us (3%)
  local copies, waits for them, and re-layouts  9.84 us (2%)
    psum x1, waiting for transfers between devices, local(): summed = lax.psum(terms, 'tok')  189 us
    psum x1, waiting for transfers between devices, local(): gram = lax.psum(local_gram, 'tok')  179 us
    psum x1, waiting for transfers between devices, local(): sampled = lax.psum(partial_rows, 'hid')  76.3 us
    another operation x10, other arithmetic, local(): lower = jnp.linalg.cholesky(gram)  50.5 us
    another operation x8, other arithmetic, local(): lax.linalg.triangular_solve(lower, sampled, left_side=False, lower=True,...  29.9 us
  transfers between devices with their start and end apart: 3, of which 3 were waited for; matrix products, arithmetic and copies ran while one was open for 0% of the time, Pallas kernels for 0%

commit v1 on v0

v1 whole, which is shorter than its diff:
```python
import functools

import jax
import jax.numpy as jnp
from jax import lax
from jax.experimental import pallas as pl
from jax.experimental.pallas import tpu as pltpu
from jax.sharding import PartitionSpec as P

MESH = pl.DeviceIdType.MESH
HI = lax.Precision.HIGHEST
F32 = jnp.float32
BF = jnp.bfloat16
K = 320
B = 64
NP = 4
PR = K // NP


def rc(src, dst, ssem, rsem, dev):
    cp = pltpu.make_async_remote_copy(
        src_ref=src, dst_ref=dst, send_sem=ssem, recv_sem=rsem, device_id=dev, device_id_type=MESH
    )
    cp.start()
    return cp


def split(v):
    hi = v.astype(BF)
    return hi, (v - hi.astype(F32)).astype(BF)


def factor(aug):
    subl = lax.broadcasted_iota(jnp.int32, (8, 128), 0)
    parts = tuple(aug[8 * i : 8 * i + 8, :] for i in range(8))

    def panel(g, parts):
        top = parts[0]
        rest = [jnp.where(g + h < 8, parts[h], 0.0) for h in range(1, 8)]
        own = [jnp.broadcast_to(top[:, j : j + 1], (8, 128)) for j in range(8)]
        cols = [[jnp.broadcast_to(p[:, j : j + 1], (8, 128)) for j in range(8)] for p in rest]
        below = list(parts[1:])
        scale = jnp.zeros((8, 128), F32)
        for t in range(8):
            row = jnp.broadcast_to(top[t : t + 1, :], (8, 128))
            piv = jnp.broadcast_to(own[t][t : t + 1, :], (8, 128))
            inv = 1.0 / piv
            scale = jnp.where(subl == t, lax.rsqrt(piv), scale)
            f = jnp.where(subl > t, own[t] * inv, 0.0)
            later = [None] * 8
            for j in range(t + 1, 8):
                later[j] = jnp.broadcast_to(own[j][t : t + 1, :], (8, 128))
                own[j] = own[j] - f * later[j]
            top = top - f * row
            for h in range(7):
                fh = cols[h][t] * inv
                for j in range(t + 1, 8):
                    cols[h][j] = cols[h][j] - fh * later[j]
                below[h] = below[h] - fh * row
        top = top * scale
        return tuple(pltpu.roll(p, 120, 1) for p in below + [top])

    return jnp.concatenate(lax.fori_loop(0, 8, panel, parts), axis=0)


def chol_step(J, n_ref):
    r0 = B * J
    tile = 128 * (J // 2)
    blk = n_ref[r0 : r0 + B, tile : tile + 128]
    if J % 2:
        blk = pltpu.roll(blk, 64, 1)
    lanes = lax.broadcasted_iota(jnp.int32, (B, 128), 1)
    rows = lax.broadcasted_iota(jnp.int32, (B, 128), 0)
    w = factor(jnp.where(lanes < B, blk, (lanes - B == rows).astype(F32)))[:, :B]
    col = lax.broadcasted_iota(jnp.int32, (B, 384), 1)
    row = lax.broadcasted_iota(jnp.int32, (B, 384), 0)
    here = (col >= r0) & (col < r0 + B)
    rin = jnp.where(here, (row + r0 == col).astype(F32), n_ref[r0 : r0 + B, :])
    r = jnp.dot(w, rin, precision=HI, preferred_element_type=F32)
    n_ref[r0 : r0 + B, :] = jnp.where(col < r0 + B, r, 0.0)
    if J < K // B - 1:
        m = K - r0 - B
        upd = lax.dot_general(r, r, (((0,), (0,)), ((), ())), precision=HI, preferred_element_type=F32)
        colb = lax.broadcasted_iota(jnp.int32, (m, 384), 1)
        old = jnp.where((colb >= r0) & (colb < r0 + B), 0.0, n_ref[r0 + B : K, :])
        n_ref[r0 + B : K, :] = old - upd[r0 + B : K, :]


def main_kernel(
    a_hbm, s_ref, samp_out, linv_out, fin_out,
    a_v, own, rsr, samp, n_ref, pk, cr, g1, xr, zb, gf, shl, ct, crx, xs, xrr, zs, zr, fin,
    a_sem, rs_s, rs_r, ag_s, ag_r, fw_s, fw_r, core_s, core_r, xy_s, xy_r, z_s, z_r, xg_s, xg_r,
    px_s, px_r, pz_s, pz_r, out_sem,
):
    t = lax.axis_index("tok")
    y = lax.axis_index("hid")
    x, z, c = t // 16, (t // 2) % 8, t % 2

    def dev(dx=0, dy=0, dz=0, dc=0):
        xx, zz, cc = lax.rem(x + dx, 4), lax.rem(z + dz, 8), lax.rem(c + dc, 2)
        return (xx * 16 + zz * 2 + cc, lax.rem(y + dy, 4))

    sends = []

    def unit(i):
        k, d = i // 2, i % 2
        q = lax.rem(y + jnp.where(d == 0, 3 - k, 1 + k), 4)
        return q * 2 + d

    def a_copy(i):
        rows = pl.ds(pl.multiple_of(unit(i) * 256, 256), 256)
        return pltpu.make_async_copy(a_hbm.at[rows], a_v.at[rows], a_sem.at[i])

    for i in range(8):
        a_copy(i).start()

    barrier = pltpu.get_barrier_semaphore()
    xy = [(dx, dy) for dx in range(4) for dy in range(4) if dx + dy]
    peers = [dev(dx=dx, dy=dy) for dx, dy in xy] + [dev(dz=d) for d in range(1, 8)] + [dev(dc=1)]
    for p in peers:
        pl.semaphore_signal(barrier, inc=1, device_id=p, device_id_type=MESH)

    def work(i):
        a_copy(i).wait()
        rows = pl.ds(pl.multiple_of(unit(i) * 256, 256), 256)
        v = lax.dot_general(
            s_ref[...], a_v[rows, :], (((1,), (1,)), ((), ())), preferred_element_type=F32
        )
        own[i // 2, i % 2] = v.reshape(NP, PR, 256)

    ydir = [dev(dy=1), dev(dy=3)]
    work(0)
    work(1)
    pl.semaphore_wait(barrier, len(peers))
    for p in range(NP):
        for d in range(2):
            sends.append(rc(own.at[0, d, p], rsr.at[d, 0, p], rs_s.at[d, 0, p], rs_r.at[d, 0, p], ydir[d]))
    arrivals = {(0, d, p): sends[2 * p + d] for p in range(NP) for d in range(2)}

    @pl.loop(2, 8)
    def _(i):
        work(i)

    def ag_send(p):
        for d in range(2):
            cp = rc(samp.at[y, p], samp.at[y, p], ag_s.at[d, p], ag_r.at[d, p], ydir[d])
            sends.append(cp)
            arrivals["ag", d, p] = cp

    for s in range(3):
        for p in range(NP):
            for d in range(2):
                arrivals[s, d, p].wait_recv()
                v = rsr[d, s, p] + own[s + 1, d, p]
                if s < 2:
                    rsr[d, s, p] = v
                    cp = rc(
                        rsr.at[d, s, p], rsr.at[d, s + 1, p], rs_s.at[d, s + 1, p], rs_r.at[d, s + 1, p], ydir[d]
                    )
                    sends.append(cp)
                    arrivals[s + 1, d, p] = cp
                else:
                    samp[y, p, d] = v
            if s == 2 and p < 2:
                ag_send(p)

    def ag_forward(p):
        for d in range(2):
            arrivals["ag", d, p].wait_recv()
            q = lax.rem(y + (3 if d == 0 else 1), 4)
            cp = rc(samp.at[q, p, d], samp.at[q, p, d], fw_s.at[d, p], fw_r.at[d, p], ydir[d])
            sends.append(cp)
            arrivals["fw", d, p] = cp

    gram = jnp.zeros((K, K), F32)
    for d in range(2):
        v = samp[y, :, d].reshape(K, 256)
        gram = gram + lax.dot_general(v, v, (((1,), (1,)), ((), ())), precision=HI, preferred_element_type=F32)
    n_ref[...] = jnp.zeros_like(n_ref)
    n_ref[:, 0:K] = gram
    low = lax.broadcasted_iota(jnp.int32, (B, 128), 1) < B

    def tile(i, j):
        return n_ref[B * i : B * i + B, 128 * j : 128 * j + 128]

    panels = [
        tile(0, 0),
        tile(0, 1),
        tile(1, 1),
        tile(2, 1),
        jnp.where(low, tile(0, 2), tile(1, 0)),
        jnp.where(low, tile(1, 2), tile(3, 1)),
        jnp.where(low, tile(2, 2), pltpu.roll(tile(3, 2), 64, 1)),
        tile(4, 2),
    ]
    for i, v in enumerate(panels):
        pk[i // 4, 4 * (i % 4) : 4 * (i % 4) + 4] = v.reshape(4, 16, 128)

    other = dev(dc=1)
    cp = rc(pk.at[1 - c], cr, core_s.at[0], core_r.at[0], other)
    sends.append(cp)
    cp.wait_recv()
    g1[...] = pk[c] + cr[...]
    me = 4 * x + y
    cps = []
    for i, (dx, dy) in enumerate(xy):
        to = 4 * lax.rem(x + dx, 4) + lax.rem(y + dy, 4)
        cps.append(rc(g1.at[to], xr.at[i], xy_s.at[i], xy_r.at[i], dev(dx=dx, dy=dy)))
    ag_send(2)
    ag_send(3)
    ag_forward(0)
    ag_forward(1)
    v = g1[me]
    for i, cp in enumerate(cps):
        cp.wait_recv()
        v = v + xr[i]
    sends += cps
    zb[z] = v
    cps = [rc(zb.at[z], zb.at[z], z_s.at[d - 1], z_r.at[d - 1], dev(dz=d)) for d in range(1, 8)]
    for cp in cps:
        cp.wait_recv()
    sends += cps
    v = zb[0]
    for i in range(1, 8):
        v = v + zb[i]
    gf[c, me] = v
    cps = [
        rc(gf.at[c, me], gf.at[c, me], xg_s.at[i], xg_r.at[i], dev(dx=dx, dy=dy)) for i, (dx, dy) in enumerate(xy)
    ]
    for cp in cps:
        cp.wait_recv()
    sends += cps
    cp = rc(gf.at[c], gf.at[c], core_s.at[1], core_r.at[1], other)
    sends.append(cp)
    cp.wait_recv()

    def panel(i):
        return gf[i // 4, 4 * (i % 4) : 4 * (i % 4) + 4].reshape(B, 128)

    def put(i, j, v):
        n_ref[B * i : B * i + B, 128 * j : 128 * j + 128] = v

    put(0, 0, panel(0))
    put(0, 1, panel(1))
    put(1, 1, panel(2))
    put(2, 1, panel(3))
    v = panel(4)
    put(0, 2, jnp.where(low, v, 0.0))
    put(1, 0, jnp.where(low, 0.0, v))
    v = panel(5)
    put(1, 2, jnp.where(low, v, 0.0))
    put(3, 1, jnp.where(low, 0.0, v))
    v = panel(6)
    put(2, 2, jnp.where(low, v, 0.0))
    put(3, 2, jnp.where(low, pltpu.roll(v, 64, 1), 0.0))
    put(4, 2, panel(7))

    def c_work(h):
        for u in range(8):
            hi, lo = split(samp[u // 2, 2 * h : 2 * h + 2, u % 2].reshape(2 * PR, 256))
            shl[0 : 2 * PR, 256 * u : 256 * u + 256] = hi
            shl[2 * PR : 4 * PR, 256 * u : 256 * u + 256] = lo

        @pl.loop(0, 8)
        def _(j):
            cols = pl.ds(pl.multiple_of(256 * j, 256), 256)
            v = jnp.dot(shl[...], a_v[:, cols], preferred_element_type=F32)
            ct[h, :, :, cols] = (v[0 : 2 * PR] + v[2 * PR : 4 * PR]).reshape(2, PR, 256)

        cp = rc(ct.at[h, 1 - c], crx.at[h], core_s.at[2 + h], core_r.at[2 + h], other)
        sends.append(cp)
        arrivals["c", h] = cp

    def x_start(h):
        arrivals["c", h].wait_recv()
        for i in range(4):
            xs[h, i] = ct[h, c, :, 512 * i : 512 * i + 512] + crx[h, :, 512 * i : 512 * i + 512]
        arrivals["x", h] = [
            rc(xs.at[h, lax.rem(x + d, 4)], xrr.at[h, d - 1], px_s.at[h, d - 1], px_r.at[h, d - 1], dev(dx=d))
            for d in range(1, 4)
        ]
        sends.extend(arrivals["x", h])

    def z_start(h):
        for cp in arrivals["x", h]:
            cp.wait_recv()
        v = xs[h, x] + xrr[h, 0] + xrr[h, 1] + xrr[h, 2]
        half = lax.broadcasted_iota(jnp.int32, (PR // 2, 128), 1) < 64
        for i in range(8):
            w = v[:, 128 * (i // 2) : 128 * (i // 2) + 128]
            top, bottom = w[0 : PR // 2], w[PR // 2 : PR]
            if i % 2:
                zs[h, i] = jnp.where(half, pltpu.roll(top, 64, 1), bottom)
            else:
                zs[h, i] = jnp.where(half, top, pltpu.roll(bottom, 64, 1))
        arrivals["z", h] = [
            rc(zs.at[h, lax.rem(z + d, 8)], zr.at[h, d - 1], pz_s.at[h, d - 1], pz_r.at[h, d - 1], dev(dz=d))
            for d in range(1, 8)
        ]
        sends.extend(arrivals["z", h])

    def z_end(h):
        v = zs[h, z]
        for i, cp in enumerate(arrivals["z", h]):
            cp.wait_recv()
            v = v + zr[h, i]
        fin[h, c] = v
        cp = rc(fin.at[h, c], fin.at[h, c], core_s.at[4 + h], core_r.at[4 + h], other)
        sends.append(cp)
        arrivals["fin", h] = cp

    def ag_end(p):
        for d in range(2):
            arrivals["fw", d, p].wait_recv()

    chol_step(0, n_ref)
    ag_forward(2)
    ag_forward(3)
    ag_end(0)
    ag_end(1)
    c_work(0)
    chol_step(1, n_ref)
    x_start(0)
    chol_step(2, n_ref)
    ag_end(2)
    ag_end(3)
    out = pltpu.make_async_copy(samp, samp_out, out_sem.at[0])
    out.start()
    c_work(1)
    x_start(1)
    z_start(0)
    chol_step(3, n_ref)
    z_end(0)
    z_start(1)
    chol_step(4, n_ref)
    linv_out[...] = n_ref[...]
    z_end(1)
    for h in range(2):
        arrivals["fin", h].wait_recv()
    out.wait()
    fin_out[...] = fin[...]
    for cp in sends:
        cp.wait_send()


def last_kernel(core, samp_ref, linv_ref, fin_ref, basis_ref, proj_ref):
    whi, wlo = split(linv_ref[:, 0:K])

    def times(v):
        hi, lo = split(v)
        dot = functools.partial(jnp.dot, preferred_element_type=F32)
        return dot(whi, hi) + (dot(whi, lo) + dot(wlo, hi))

    basis_ref[...] = times(samp_ref[0, :, 0].reshape(K, 256))

    @pl.when(pl.program_id(0) == 0)
    def _():
        rows = []
        for p in range(NP):
            v = fin_ref[p // 2, p % 2]
            rows += [v, pltpu.roll(v, 64, 1)]
        v = jnp.transpose(times(jnp.concatenate(rows, axis=0)))
        proj_ref[...] = jnp.where(core[0] == 0, v[0:32], v[32:64])


def local(activations, sketch):
    dma = pltpu.SemaphoreType.DMA
    vm = pltpu.VMEM
    samp, linv, fin = pl.pallas_call(
        main_kernel,
        out_shape=(
            jax.ShapeDtypeStruct((4, NP, 2, PR, 256), F32),
            jax.ShapeDtypeStruct((K, 384), F32),
            jax.ShapeDtypeStruct((2, 2, PR // 2, 128), F32),
        ),
        in_specs=[pl.BlockSpec(memory_space=pl.ANY), pl.BlockSpec(memory_space=vm)],
        out_specs=(
            pl.BlockSpec(memory_space=pl.ANY),
            pl.BlockSpec(memory_space=vm),
            pl.BlockSpec(memory_space=vm),
        ),
        scratch_shapes=[
            vm((2048, 2048), BF),
            vm((4, 2, NP, PR, 256), F32),
            vm((2, 3, NP, PR, 256), F32),
            vm((4, NP, 2, PR, 256), F32),
            vm((K, 384), F32),
            vm((2, 16, 16, 128), F32),
            vm((16, 16, 128), F32),
            vm((16, 16, 128), F32),
            vm((15, 16, 128), F32),
            vm((8, 16, 128), F32),
            vm((2, 16, 16, 128), F32),
            vm((4 * PR, 2048), BF),
            vm((2, 2, PR, 2048), F32),
            vm((2, PR, 2048), F32),
            vm((2, 4, PR, 512), F32),
            vm((2, 3, PR, 512), F32),
            vm((2, 8, PR // 2, 128), F32),
            vm((2, 7, PR // 2, 128), F32),
            vm((2, 2, PR // 2, 128), F32),
            dma((8,)),
            dma((2, 3, NP)),
            dma((2, 3, NP)),
            dma((2, NP)),
            dma((2, NP)),
            dma((2, NP)),
            dma((2, NP)),
            dma((6,)),
            dma((6,)),
            dma((15,)),
            dma((15,)),
            dma((7,)),
            dma((7,)),
            dma((15,)),
            dma((15,)),
            dma((2, 3)),
            dma((2, 3)),
            dma((2, 7)),
            dma((2, 7)),
            dma((1,)),
        ],
        compiler_params=pltpu.CompilerParams(
            collective_id=0, has_side_effects=True, vmem_limit_bytes=56 * 1024 * 1024
        ),
        name="main",
    )(activations, sketch.T)
    core = (lax.axis_index("tok") % 2).astype(jnp.int32).reshape(1)
    basis, proj = pl.pallas_call(
        last_kernel,
        grid_spec=pltpu.PrefetchScalarGridSpec(
            num_scalar_prefetch=1,
            grid=(8,),
            in_specs=[
                pl.BlockSpec((1, NP, 1, PR, 256), lambda i, core: (i // 2, 0, i % 2, 0, 0)),
                pl.BlockSpec((K, 384), lambda i, core: (0, 0)),
                pl.BlockSpec((2, 2, PR // 2, 128), lambda i, core: (0, 0, 0, 0)),
            ],
            out_specs=[
                pl.BlockSpec((K, 256), lambda i, core: (0, i)),
                pl.BlockSpec((32, K), lambda i, core: (0, 0)),
            ],
        ),
        out_shape=(jax.ShapeDtypeStruct((K, 2048), F32), jax.ShapeDtypeStruct((32, K), F32)),
        compiler_params=pltpu.CompilerParams(vmem_limit_bytes=32 * 1024 * 1024),
        name="last",
    )(core, samp, linv, fin)
    return basis.T, proj


def solution(mesh):
    in_specs = (P("tok", "hid"), P("hid", None))
    out_specs = (P("tok", None), P(("hid", "tok"), None))
    return jax.shard_map(local, mesh=mesh, in_specs=in_specs, out_specs=out_specs, check_vma=False)
```

time: 583 us -> 107 us (0.18)
  waiting for transfers between devices: 444 us -> 0 us
  Pallas kernels: 0 us -> 102 us
  other arithmetic: 81.5 us -> 0 us
  matrix products: 29.8 us -> 0 us
  between operations: 15.9 us -> 0.66 us
  local copies, waits for them, and re-layouts: 9.84 us -> 3.65 us
    psum x3 -> x0, waiting for transfers between devices: 444 us -> none  [the longest x1 189 us: local(): summed = lax.psum(terms, 'tok')]
    pallas_call x0 -> x2, Pallas kernels: none -> 102 us  [the longest x1 96.6 us: local(): pl.pallas_call(main_kernel, out_shape=(jax.ShapeDtypeStruct((4, NP, 2, PR...]
    another operation x18 -> x0, other arithmetic: 80.4 us -> none  [the longest x10 50.5 us: local(): lower = jnp.linalg.cholesky(gram)]
    dot_general x3 -> x0, matrix products: 19.7 us -> none  [the longest x1 7.78 us: local(): jnp.dot(activations, sketch, preferred_element_type=jnp.float32)]
    another operation x9 -> x0, matrix products: 10 us -> none  [the longest x5 9.12 us: local(): lax.linalg.triangular_solve(lower, sampled, left_side=False, lower=True,...]
  transfers between devices with their start and end apart: 3 -> 0, of which waited for: 3 -> 0; matrix products, arithmetic and copies ran while one was open for 0% -> 0% of each run, Pallas kernels for 0% -> 0%
where the time goes in v1:
time: 107 us; the launch traced here: 106 us
  Pallas kernels  102 us (95%)
  local copies, waits for them, and re-layouts  3.65 us (3%)
    pallas_call x1, Pallas kernels, local(): pl.pallas_call(main_kernel, out_shape=(jax.ShapeDtypeStruct((4, NP, 2, PR...  96.6 us
    pallas_call x1, Pallas kernels, local(): pl.pallas_call(last_kernel, grid_spec=pltpu.PrefetchScalarGridSpec(num_sc...  5.58 us
    unnamed x6, local copies, waits for them, and re-layouts  3.65 us

profile of v1, /device:TPU:1, one launch (start us, length us, event | category | flops | bytes accessed | tf_op | source)
XLA Modules:
  0.0 106.5 jit_solution(15876313491575912604)
XLA Ops:
  0.6 96.6 %main.1 = (f32[4,4,2,80,256]{4,3,2,1,0:T(8,128)}, f32[320,384]{1,0:T(8,128)}, f32[2,2,40,128]{3,2,1,0:T(8,128)}) custom-call(bf16[2048,2048]{1,0:T(8,128)(2,1)} %a_hbm.1, bf16[320,2048]{1,0:T(8,128)(2,1)} %bitcast.3), custom_call_target="tpu_custom_call" | custom-call | tf_op jit(solution)/shard_map/main/pallas_call | solution.py:369
  97.3 0.0 copy-start
  97.3 1.7 %copy-done = f32[4,4,2,80,256]{4,3,2,1,0:T(8,128)S(1)} copy-done((f32[4,4,2,80,256]{4,3,2,1,0:T(8,128)S(1)}, f32[4,4,2,80,256]{4,3,2,1,0:T(8,128)}, u32[]{:S(2)}) %copy-start) | copy-done | bytes 2621464
  99.0 0.0 copy-start.1
  99.0 1.0 copy-done.1
  100.0 0.0 copy-start.2
  100.0 0.9 copy-done.2
  100.9 5.6 %last.1 = (f32[320,2048]{1,0:T(8,128)}, f32[32,320]{1,0:T(8,128)}) custom-call(s32[1]{0:T(128)} %bitcast.core, f32[4,4,2,80,256]{4,3,2,1,0:T(8,128)S(1)} %copy-done, f32[320,384]{1,0:T(8,128)S(1)} %copy-done.1, f32[2,2,40,128]{3,2,1,0:T(8,128)S(1)} %copy-done.2), custom_call_target="tpu_custom_call" | custom-call | tf_op jit(solution)/shard_map/last/pallas_call | solution.py:429
Async XLA Ops:
  97.3 1.7 %copy-start = (f32[4,4,2,80,256]{4,3,2,1,0:T(8,128)S(1)}, f32[4,4,2,80,256]{4,3,2,1,0:T(8,128)}, u32[]{:S(2)}) copy-start(f32[4,4,2,80,256]{4,3,2,1,0:T(8,128)} %get-tuple-element.7.samp_ref) | copy-start | bytes 7864324
  99.0 1.0 copy-start.1
  100.0 0.9 copy-start.2

commit v2 on v1

v2 whole, which is shorter than its diff:
```python
import functools

import jax
import jax.numpy as jnp
from jax import lax
from jax.experimental import pallas as pl
from jax.experimental.pallas import tpu as pltpu
from jax.sharding import PartitionSpec as P

MESH = pl.DeviceIdType.MESH
HI = lax.Precision.HIGHEST
F32 = jnp.float32
BF = jnp.bfloat16
K = 320
B = 64
NP = 5
PR = K // NP
GROUPS = ((0, 2), (2, 4), (4, 5))
SIZES = tuple((b - a) * PR // 2 for a, b in GROUPS)


def rc(src, dst, ssem, rsem, dev):
    cp = pltpu.make_async_remote_copy(
        src_ref=src, dst_ref=dst, send_sem=ssem, recv_sem=rsem, device_id=dev, device_id_type=MESH
    )
    cp.start()
    return cp


def split(v):
    hi = v.astype(BF)
    return hi, (v - hi.astype(F32)).astype(BF)


def factor(aug):
    subl = lax.broadcasted_iota(jnp.int32, (8, 128), 0)
    w = 16
    n = w // 8

    def spread(v, i):
        return jnp.broadcast_to(v[i : i + 1, :], (8, 128))

    parts = [aug[8 * i : 8 * i + 8, :] for i in range(8)]
    for g in range(0, 8, n):
        cur = parts[g:]
        cols = [[jnp.broadcast_to(v[:, 8 * g + j : 8 * g + j + 1], (8, 128)) for j in range(w)] for v in cur]
        scale = [jnp.zeros((8, 128), F32) for _ in range(n)]
        for t in range(w):
            o, i = t // 8, t % 8
            piv = spread(cols[o][t], i)
            inv = 1.0 / piv
            scale[o] = jnp.where(subl == i, lax.rsqrt(piv), scale[o])
            row = spread(cur[o], i)
            later = {j: spread(cols[o][j], i) for j in range(t + 1, w)}
            for h in range(o, len(cur)):
                f = cols[h][t] * inv
                if h == o:
                    f = jnp.where(subl > i, f, 0.0)
                for j in range(t + 1, w):
                    cols[h][j] = cols[h][j] - f * later[j]
                cur[h] = cur[h] - f * row
        parts = parts[:g] + [cur[o] * scale[o] for o in range(n)] + cur[n:]
    return jnp.concatenate(parts, axis=0)


def chol_step(J, n_ref):
    r0 = B * J
    tile = 128 * (J // 2)
    blk = n_ref[r0 : r0 + B, tile : tile + 128]
    if J % 2:
        blk = pltpu.roll(blk, 64, 1)
    lanes = lax.broadcasted_iota(jnp.int32, (B, 128), 1)
    rows = lax.broadcasted_iota(jnp.int32, (B, 128), 0)
    w = pltpu.roll(factor(jnp.where(lanes < B, blk, (lanes - B == rows).astype(F32))), 64, 1)[:, :B]
    col = lax.broadcasted_iota(jnp.int32, (B, 384), 1)
    row = lax.broadcasted_iota(jnp.int32, (B, 384), 0)
    here = (col >= r0) & (col < r0 + B)
    rin = jnp.where(here, (row + r0 == col).astype(F32), n_ref[r0 : r0 + B, :])
    r = jnp.dot(w, rin, precision=HI, preferred_element_type=F32)
    n_ref[r0 : r0 + B, :] = jnp.where(col < r0 + B, r, 0.0)
    if J < K // B - 1:
        m = K - r0 - B
        upd = lax.dot_general(r, r, (((0,), (0,)), ((), ())), precision=HI, preferred_element_type=F32)
        colb = lax.broadcasted_iota(jnp.int32, (m, 384), 1)
        old = jnp.where((colb >= r0) & (colb < r0 + B), 0.0, n_ref[r0 + B : K, :])
        n_ref[r0 + B : K, :] = old - upd[r0 + B : K, :]


def main_kernel(
    a_hbm, s_hbm, bs, proj_out,
    a_v, s_ref, own, rsr, samp, n_ref, pk, cr, g1, xr, zb, gf, shl,
    ct0, ct1, ct2, crx0, crx1, crx2, xs0, xs1, xs2, xrr0, xrr1, xrr2, zs0, zs1, zs2, zr0, zr1, zr2,
    fin0, fin1, fin2,
    a_sem, rs_s, rs_r, ag_s, ag_r, fw_s, fw_r, core_s, core_r, xy_s, xy_r, z_s, z_r, xg_s, xg_r,
    px_s, px_r, pz_s, pz_r,
):
    ct, crx, xs, xrr = (ct0, ct1, ct2), (crx0, crx1, crx2), (xs0, xs1, xs2), (xrr0, xrr1, xrr2)
    zs, zr, fin = (zs0, zs1, zs2), (zr0, zr1, zr2), (fin0, fin1, fin2)
    t = lax.axis_index("tok")
    y = lax.axis_index("hid")
    x, z, c = t // 16, (t // 2) % 8, t % 2

    def dev(dx=0, dy=0, dz=0, dc=0):
        xx, zz, cc = lax.rem(x + dx, 4), lax.rem(z + dz, 8), lax.rem(c + dc, 2)
        return (xx * 16 + zz * 2 + cc, lax.rem(y + dy, 4))

    sends = []

    def unit(i):
        k, d = i // 2, i % 2
        q = lax.rem(y + jnp.where(d == 0, 3 - k, 1 + k), 4)
        return q * 2 + d

    def a_copy(i):
        rows = pl.ds(pl.multiple_of(unit(i) * 256, 256), 256)
        return pltpu.make_async_copy(a_hbm.at[rows], a_v.at[rows], a_sem.at[i])

    barrier = pltpu.get_barrier_semaphore()
    xy = [(dx, dy) for dx in range(4) for dy in range(4) if dx + dy]
    peers = [dev(dy=1), dev(dy=3), dev(dc=1)] + [dev(dz=d) for d in range(1, 8)]
    peers += [dev(dx=dx, dy=dy) for dx, dy in xy if (dx, dy) not in ((0, 1), (0, 3))]
    for p in peers:
        pl.semaphore_signal(barrier, inc=1, device_id=p, device_id_type=MESH)
    s_copy = pltpu.make_async_copy(s_hbm, s_ref, a_sem.at[8])
    s_copy.start()
    a_copy(0).start()
    a_copy(1).start()
    s_copy.wait()

    def work(i, ahead=()):
        a_copy(i).wait()
        for j in ahead:
            a_copy(j).start()
        rows = pl.ds(pl.multiple_of(unit(i) * 256, 256), 256)
        v = lax.dot_general(
            s_ref[...], a_v[rows, :], (((1,), (1,)), ((), ())), preferred_element_type=F32
        )
        own[i // 2, i % 2] = v.reshape(NP, PR, 256)

    ydir = [dev(dy=1), dev(dy=3)]
    work(0, range(2, 4))
    work(1, range(4, 8))
    pl.semaphore_wait(barrier, len(peers))
    for p in range(NP):
        for d in range(2):
            sends.append(rc(own.at[0, d, p], rsr.at[d, 0, p], rs_s.at[d, 0, p], rs_r.at[d, 0, p], ydir[d]))
    arrivals = {(0, d, p): sends[2 * p + d] for p in range(NP) for d in range(2)}

    @pl.loop(2, 8)
    def _(i):
        work(i)

    def ag_send(p):
        for d in range(2):
            cp = rc(samp.at[y, p], samp.at[y, p], ag_s.at[d, p], ag_r.at[d, p], ydir[d])
            sends.append(cp)
            arrivals["ag", d, p] = cp

    def gram(p):
        v = None
        for d in range(2):
            u = lax.dot_general(
                samp[y, 0 : p + 1, d].reshape((p + 1) * PR, 256),
                samp[y, p, d],
                (((1,), (1,)), ((), ())),
                precision=HI,
                preferred_element_type=F32,
            )
            v = u if v is None else v + u
        n_ref[0 : (p + 1) * PR, p * PR : (p + 1) * PR] = v

    n_ref[...] = jnp.zeros_like(n_ref)
    for s in range(3):
        for p in range(NP):
            for d in range(2):
                arrivals[s, d, p].wait_recv()
                v = rsr[d, s, p] + own[s + 1, d, p]
                if s < 2:
                    rsr[d, s, p] = v
                    cp = rc(
                        rsr.at[d, s, p], rsr.at[d, s + 1, p], rs_s.at[d, s + 1, p], rs_r.at[d, s + 1, p], ydir[d]
                    )
                    sends.append(cp)
                    arrivals[s + 1, d, p] = cp
                else:
                    samp[y, p, d] = v
            if s == 2:
                if p < 3:
                    ag_send(p)
                gram(p)

    def ag_forward(p):
        for d in range(2):
            arrivals["ag", d, p].wait_recv()
            q = lax.rem(y + (3 if d == 0 else 1), 4)
            cp = rc(samp.at[q, p, d], samp.at[q, p, d], fw_s.at[d, p], fw_r.at[d, p], ydir[d])
            sends.append(cp)
            arrivals["fw", d, p] = cp

    def ag_end(p):
        for d in range(2):
            arrivals["fw", d, p].wait_recv()

    ring = (0, 1, 3, 2)

    def c_part(h, steps, first):
        a, b = GROUPS[h]
        r = 2 * SIZES[h]
        for i in steps:
            q = lax.rem(y + ring[i], 4)
            for d in range(2):
                hi, lo = split(samp[q, a:b, d].reshape(r, 256))
                shl[i, 0:r, 256 * d : 256 * d + 256] = hi
                shl[i, r : 2 * r, 256 * d : 256 * d + 256] = lo

        @pl.loop(0, 4)
        def _(j):
            cols = pl.ds(pl.multiple_of(512 * j, 512), 512)
            v = None
            for i in steps:
                rows = pl.ds(pl.multiple_of(512 * lax.rem(y + ring[i], 4), 512), 512)
                u = jnp.dot(shl[i, 0 : 2 * r], a_v[rows, cols], preferred_element_type=F32)
                v = u if v is None else v + u
            v = (v[0:r] + v[r : 2 * r]).reshape(2, r // 2, 512)
            ct[h][:, :, cols] = v if first else ct[h][:, :, cols] + v

    def c_send(h):
        cp = rc(ct[h].at[1 - c], crx[h], core_s.at[2 + h], core_r.at[2 + h], dev(dc=1))
        sends.append(cp)
        arrivals["c", h] = cp

    def c_work(h):
        c_part(h, range(4), True)
        c_send(h)

    def x_start(h):
        arrivals["c", h].wait_recv()
        for i in range(4):
            xs[h][i] = ct[h][c, :, 512 * i : 512 * i + 512] + crx[h][:, 512 * i : 512 * i + 512]
        arrivals["x", h] = [
            rc(xs[h].at[lax.rem(x + d, 4)], xrr[h].at[d - 1], px_s.at[h, d - 1], px_r.at[h, d - 1], dev(dx=d))
            for d in range(1, 4)
        ]
        sends.extend(arrivals["x", h])

    def z_start(h):
        for cp in arrivals["x", h]:
            cp.wait_recv()
        v = xs[h][x] + xrr[h][0] + xrr[h][1] + xrr[h][2]
        n = SIZES[h] // 2
        half = lax.broadcasted_iota(jnp.int32, (n, 128), 1) < 64
        for i in range(8):
            w = v[:, 128 * (i // 2) : 128 * (i // 2) + 128]
            top, bottom = w[0:n], w[n : 2 * n]
            if i % 2:
                zs[h][i] = jnp.where(half, pltpu.roll(top, 64, 1), bottom)
            else:
                zs[h][i] = jnp.where(half, top, pltpu.roll(bottom, 64, 1))
        arrivals["z", h] = [
            rc(zs[h].at[lax.rem(z + d, 8)], zr[h].at[d - 1], pz_s.at[h, d - 1], pz_r.at[h, d - 1], dev(dz=d))
            for d in range(1, 8)
        ]
        sends.extend(arrivals["z", h])

    def z_end(h):
        v = zs[h][z]
        for i, cp in enumerate(arrivals["z", h]):
            cp.wait_recv()
            v = v + zr[h][i]
        fin[h][c] = v
        cp = rc(fin[h].at[c], fin[h].at[c], core_s.at[5 + h], core_r.at[5 + h], dev(dc=1))
        sends.append(cp)
        arrivals["fin", h] = cp

    dot = functools.partial(jnp.dot, preferred_element_type=F32)

    def basis():
        whi, wlo = split(n_ref[:, 0:K])
        both = jnp.concatenate([whi[0:256, 0:256], wlo[0:256, 0:256]], axis=0)
        low = jnp.concatenate([whi[256:K], wlo[256:K]], axis=0)

        @pl.loop(0, 8)
        def _(u):
            hi, lo = split(samp[u // 2, :, u % 2].reshape(K, 256))
            cols = pl.ds(pl.multiple_of(256 * u, 256), 256)
            v = dot(both, hi[0:256])
            bs[0:256, cols] = v[0:256] + (v[256:512] + dot(whi[0:256, 0:256], lo[0:256]))
            v = dot(low, hi)
            bs[256:K, cols] = v[0:64] + (v[64:128] + dot(whi[256:K], lo))

    def projected():
        for h in range(len(GROUPS)):
            arrivals["fin", h].wait_recv()
        rows = []
        for h in range(len(GROUPS)):
            for i in range(2):
                rows += [fin[h][i], pltpu.roll(fin[h][i], 64, 1)]
        v = jnp.dot(n_ref[:, 0:K], jnp.concatenate(rows, axis=0), precision=HI, preferred_element_type=F32)
        v = jnp.transpose(v)
        proj_out[...] = jnp.where(c == 0, v[0:32], v[32:64])

    low = lax.broadcasted_iota(jnp.int32, (B, 128), 1) < B

    def tile(i, j):
        return n_ref[B * i : B * i + B, 128 * j : 128 * j + 128]

    panels = [
        tile(0, 0),
        tile(0, 1),
        tile(1, 1),
        tile(2, 1),
        jnp.where(low, tile(0, 2), tile(1, 0)),
        jnp.where(low, tile(1, 2), tile(3, 1)),
        jnp.where(low, tile(2, 2), pltpu.roll(tile(3, 2), 64, 1)),
        tile(4, 2),
    ]
    for i, v in enumerate(panels):
        pk[i // 4, 4 * (i % 4) : 4 * (i % 4) + 4] = v.reshape(4, 16, 128)

    other = dev(dc=1)
    cp = rc(pk.at[1 - c], cr, core_s.at[0], core_r.at[0], other)
    sends.append(cp)
    cp.wait_recv()
    g1[...] = pk[c] + cr[...]
    me = 4 * x + y
    cps = []
    for i, (dx, dy) in enumerate(xy):
        to = 4 * lax.rem(x + dx, 4) + lax.rem(y + dy, 4)
        cps.append(rc(g1.at[to], xr.at[i], xy_s.at[i], xy_r.at[i], dev(dx=dx, dy=dy)))
    ag_forward(0)
    ag_send(3)
    v = g1[me]
    for i, cp in enumerate(cps):
        cp.wait_recv()
        v = v + xr[i]
    sends += cps
    zb[z] = v
    cps = [rc(zb.at[z], zb.at[z], z_s.at[d - 1], z_r.at[d - 1], dev(dz=d)) for d in range(1, 8)]
    ag_forward(1)
    ag_send(4)
    for cp in cps:
        cp.wait_recv()
    sends += cps
    v = zb[0]
    for i in range(1, 8):
        v = v + zb[i]
    gf[c, me] = v
    cps = [
        rc(gf.at[c, me], gf.at[c, me], xg_s.at[i], xg_r.at[i], dev(dx=dx, dy=dy)) for i, (dx, dy) in enumerate(xy)
    ]
    sends += cps
    ag_forward(2)
    ag_forward(3)
    ag_end(0)
    ag_end(1)
    c_work(0)
    for cp in cps:
        cp.wait_recv()
    cp = rc(gf.at[c], gf.at[c], core_s.at[1], core_r.at[1], other)
    sends.append(cp)
    ag_forward(4)
    cp.wait_recv()

    def panel(i):
        return gf[i // 4, 4 * (i % 4) : 4 * (i % 4) + 4].reshape(B, 128)

    def put(i, j, v):
        n_ref[B * i : B * i + B, 128 * j : 128 * j + 128] = v

    put(0, 0, panel(0))
    put(0, 1, panel(1))
    put(1, 1, panel(2))
    put(2, 1, panel(3))
    v = panel(4)
    put(0, 2, jnp.where(low, v, 0.0))
    put(1, 0, jnp.where(low, 0.0, v))
    v = panel(5)
    put(1, 2, jnp.where(low, v, 0.0))
    put(3, 1, jnp.where(low, 0.0, v))
    v = panel(6)
    put(2, 2, jnp.where(low, v, 0.0))
    put(3, 2, jnp.where(low, pltpu.roll(v, 64, 1), 0.0))
    put(4, 2, panel(7))

    x_start(0)
    ag_end(2)
    ag_end(3)
    c_work(1)
    ag_end(4)
    c_work(2)
    x_start(1)
    z_start(0)
    chol_step(0, n_ref)
    x_start(2)
    chol_step(1, n_ref)
    z_end(0)
    z_start(1)
    chol_step(2, n_ref)
    z_start(2)
    chol_step(3, n_ref)
    z_end(1)
    chol_step(4, n_ref)
    z_end(2)
    basis()
    projected()
    for cp in sends:
        cp.wait_send()


def local(activations, sketch):
    dma = pltpu.SemaphoreType.DMA
    vm = pltpu.VMEM
    n = len(GROUPS)
    basis, proj = pl.pallas_call(
        main_kernel,
        out_shape=(vm((K, 2048), F32), vm((32, K), F32)),
        in_specs=[pl.BlockSpec(memory_space=pl.ANY)] * 2,
        out_specs=(pl.BlockSpec(memory_space=vm), pl.BlockSpec(memory_space=vm)),
        scratch_shapes=[
            vm((2048, 2048), BF),
            vm((K, 2048), BF),
            vm((4, 2, NP, PR, 256), F32),
            vm((2, 3, NP, PR, 256), F32),
            vm((4, NP, 2, PR, 256), F32),
            vm((K, 384), F32),
            vm((2, 16, 16, 128), F32),
            vm((16, 16, 128), F32),
            vm((16, 16, 128), F32),
            vm((15, 16, 128), F32),
            vm((8, 16, 128), F32),
            vm((2, 16, 16, 128), F32),
            vm((4, 4 * max(SIZES), 512), BF),
            *[vm((2, r, 2048), F32) for r in SIZES],
            *[vm((r, 2048), F32) for r in SIZES],
            *[vm((4, r, 512), F32) for r in SIZES],
            *[vm((3, r, 512), F32) for r in SIZES],
            *[vm((8, r // 2, 128), F32) for r in SIZES],
            *[vm((7, r // 2, 128), F32) for r in SIZES],
            *[vm((2, r // 2, 128), F32) for r in SIZES],
            dma((9,)),
            dma((2, 3, NP)),
            dma((2, 3, NP)),
            dma((2, NP)),
            dma((2, NP)),
            dma((2, NP)),
            dma((2, NP)),
            dma((2 + 2 * n,)),
            dma((2 + 2 * n,)),
            dma((15,)),
            dma((15,)),
            dma((7,)),
            dma((7,)),
            dma((15,)),
            dma((15,)),
            dma((n, 3)),
            dma((n, 3)),
            dma((n, 7)),
            dma((n, 7)),
        ],
        compiler_params=pltpu.CompilerParams(
            collective_id=0, has_side_effects=True, vmem_limit_bytes=58 * 1024 * 1024
        ),
        name="main",
    )(activations, sketch.T)
    return basis.T, proj


def solution(mesh):
    in_specs = (P("tok", "hid"), P("hid", None))
    out_specs = (P("tok", None), P(("hid", "tok"), None))
    return jax.shard_map(local, mesh=mesh, in_specs=in_specs, out_specs=out_specs, check_vma=False)
```

time: 107 us -> 87.7 us (0.82)
  Pallas kernels: 102 us -> 84.9 us
  local copies, waits for them, and re-layouts: 3.65 us -> 2.11 us
    pallas_call x2 -> x1, Pallas kernels: 102 us -> 84.9 us  [local(): pl.pallas_call(main_kernel, out_shape=(vm((K, 2048), F32), vm((32, K), F3...]
    unnamed x6 -> x2, local copies, waits for them, and re-layouts: 3.65 us -> 2.11 us
where the time goes in v2:
time: 87.7 us; the launch traced here: 87.6 us
  Pallas kernels  84.9 us (97%)
  local copies, waits for them, and re-layouts  2.11 us (2%)
    pallas_call x1, Pallas kernels, local(): pl.pallas_call(main_kernel, out_shape=(vm((K, 2048), F32), vm((32, K), F3...  84.9 us
    unnamed x2, local copies, waits for them, and re-layouts  2.11 us

profile of v2, /device:TPU:1, one launch (start us, length us, event | category | flops | bytes accessed | tf_op | source)
XLA Modules:
  0.0 87.6 jit_solution(2553052061563618088)
XLA Ops:
  0.6 84.9 %main.1 = (f32[320,2048]{1,0:T(8,128)S(1)}, f32[32,320]{1,0:T(8,128)S(1)}) custom-call(bf16[2048,2048]{1,0:T(8,128)(2,1)} %a_hbm.1, bf16[320,2048]{1,0:T(8,128)(2,1)} %bitcast.3), custom_call_target="tpu_custom_call" | custom-call | tf_op jit(solution)/shard_map/main/pallas_call | solution.py:414
  85.5 1.5 %copy.6 = f32[2048,320]{0,1:T(8,128)} copy(f32[2048,320]{0,1:T(8,128)S(1)} %bitcast.2) | data formatting | bytes 5242880
  87.0 0.6 copy.7

commit v3 on v2

--- a/solution.py
+++ b/solution.py
@@ -15,7 +15,7 @@
 B = 64
 NP = 5
 PR = K // NP
-GROUPS = ((0, 2), (2, 4), (4, 5))
+GROUPS = ((0, 3), (3, 5))
 SIZES = tuple((b - a) * PR // 2 for a, b in GROUPS)
 
 
@@ -89,13 +89,12 @@
 def main_kernel(
     a_hbm, s_hbm, bs, proj_out,
     a_v, s_ref, own, rsr, samp, n_ref, pk, cr, g1, xr, zb, gf, shl,
-    ct0, ct1, ct2, crx0, crx1, crx2, xs0, xs1, xs2, xrr0, xrr1, xrr2, zs0, zs1, zs2, zr0, zr1, zr2,
-    fin0, fin1, fin2,
+    ct0, ct1, crx0, crx1, xs0, xs1, xrr0, xrr1, zs0, zs1, zr0, zr1, fin0, fin1,
     a_sem, rs_s, rs_r, ag_s, ag_r, fw_s, fw_r, core_s, core_r, xy_s, xy_r, z_s, z_r, xg_s, xg_r,
     px_s, px_r, pz_s, pz_r,
 ):
-    ct, crx, xs, xrr = (ct0, ct1, ct2), (crx0, crx1, crx2), (xs0, xs1, xs2), (xrr0, xrr1, xrr2)
-    zs, zr, fin = (zs0, zs1, zs2), (zr0, zr1, zr2), (fin0, fin1, fin2)
+    ct, crx, xs, xrr = (ct0, ct1), (crx0, crx1), (xs0, xs1), (xrr0, xrr1)
+    zs, zr, fin = (zs0, zs1), (zr0, zr1), (fin0, fin1)
     t = lax.axis_index("tok")
     y = lax.axis_index("hid")
     x, z, c = t // 16, (t // 2) % 8, t % 2
@@ -268,18 +267,18 @@
             cp.wait_recv()
             v = v + zr[h][i]
         fin[h][c] = v
-        cp = rc(fin[h].at[c], fin[h].at[c], core_s.at[5 + h], core_r.at[5 + h], dev(dc=1))
+        cp = rc(fin[h].at[c], fin[h].at[c], core_s.at[4 + h], core_r.at[4 + h], dev(dc=1))
         sends.append(cp)
         arrivals["fin", h] = cp
 
     dot = functools.partial(jnp.dot, preferred_element_type=F32)
 
-    def basis():
+    def basis(first, last):
         whi, wlo = split(n_ref[:, 0:K])
         both = jnp.concatenate([whi[0:256, 0:256], wlo[0:256, 0:256]], axis=0)
         low = jnp.concatenate([whi[256:K], wlo[256:K]], axis=0)
 
-        @pl.loop(0, 8)
+        @pl.loop(first, last)
         def _(u):
             hi, lo = split(samp[u // 2, :, u % 2].reshape(K, 256))
             cols = pl.ds(pl.multiple_of(256 * u, 256), 256)
@@ -338,6 +337,7 @@
     cps = [rc(zb.at[z], zb.at[z], z_s.at[d - 1], z_r.at[d - 1], dev(dz=d)) for d in range(1, 8)]
     ag_forward(1)
     ag_send(4)
+    ag_forward(2)
     for cp in cps:
         cp.wait_recv()
     sends += cps
@@ -349,10 +349,10 @@
         rc(gf.at[c, me], gf.at[c, me], xg_s.at[i], xg_r.at[i], dev(dx=dx, dy=dy)) for i, (dx, dy) in enumerate(xy)
     ]
     sends += cps
-    ag_forward(2)
     ag_forward(3)
     ag_end(0)
     ag_end(1)
+    ag_end(2)
     c_work(0)
     for cp in cps:
         cp.wait_recv()
@@ -383,25 +383,21 @@
     put(4, 2, panel(7))
 
     x_start(0)
-    ag_end(2)
     ag_end(3)
+    ag_end(4)
     c_work(1)
-    ag_end(4)
-    c_work(2)
     x_start(1)
+    chol_step(0, n_ref)
     z_start(0)
-    chol_step(0, n_ref)
-    x_start(2)
     chol_step(1, n_ref)
+    chol_step(2, n_ref)
+    z_start(1)
     z_end(0)
-    z_start(1)
-    chol_step(2, n_ref)
-    z_start(2)
     chol_step(3, n_ref)
+    chol_step(4, n_ref)
+    basis(0, 4)
     z_end(1)
-    chol_step(4, n_ref)
-    z_end(2)
-    basis()
+    basis(4, 8)
     projected()
     for cp in sends:
         cp.wait_send()

time: 87.7 us -> 93.3 us (1.064)
  Pallas kernels: 84.9 us -> 90.4 us
    pallas_call x1, Pallas kernels: 84.9 us -> 90.4 us  [local(): pl.pallas_call(main_kernel, out_shape=(vm((K, 2048), F32), vm((32, K), F3...]
where the time goes in v3:
time: 93.3 us; the launch traced here: 93.2 us
  Pallas kernels  90.4 us (97%)
  local copies, waits for them, and re-layouts  2.11 us (2%)
    pallas_call x1, Pallas kernels, local(): pl.pallas_call(main_kernel, out_shape=(vm((K, 2048), F32), vm((32, K), F3...  90.4 us
    unnamed x2, local copies, waits for them, and re-layouts  2.11 us

profile of v3, /device:TPU:1, one launch (start us, length us, event | category | flops | bytes accessed | tf_op | source)
XLA Modules:
  0.0 93.2 jit_solution(17722672228889988413)
XLA Ops:
  0.6 90.4 %main.1 = (f32[320,2048]{1,0:T(8,128)S(1)}, f32[32,320]{1,0:T(8,128)S(1)}) custom-call(bf16[2048,2048]{1,0:T(8,128)(2,1)} %a_hbm.1, bf16[320,2048]{1,0:T(8,128)(2,1)} %bitcast.3), custom_call_target="tpu_custom_call" | custom-call | tf_op jit(solution)/shard_map/main/pallas_call | solution.py:410
  91.1 1.5 %copy.6 = f32[2048,320]{0,1:T(8,128)} copy(f32[2048,320]{0,1:T(8,128)S(1)} %bitcast.2) | data formatting | bytes 5242880
  92.6 0.6 copy.7

commit v4 on v2

--- a/solution.py
+++ b/solution.py
@@ -185,8 +185,7 @@
                 else:
                     samp[y, p, d] = v
             if s == 2:
-                if p < 3:
-                    ag_send(p)
+                ag_send(p)
                 gram(p)
 
     def ag_forward(p):
@@ -274,12 +273,12 @@
 
     dot = functools.partial(jnp.dot, preferred_element_type=F32)
 
-    def basis():
+    def basis(first, last):
         whi, wlo = split(n_ref[:, 0:K])
         both = jnp.concatenate([whi[0:256, 0:256], wlo[0:256, 0:256]], axis=0)
         low = jnp.concatenate([whi[256:K], wlo[256:K]], axis=0)
 
-        @pl.loop(0, 8)
+        @pl.loop(first, last)
         def _(u):
             hi, lo = split(samp[u // 2, :, u % 2].reshape(K, 256))
             cols = pl.ds(pl.multiple_of(256 * u, 256), 256)
@@ -328,7 +327,6 @@
         to = 4 * lax.rem(x + dx, 4) + lax.rem(y + dy, 4)
         cps.append(rc(g1.at[to], xr.at[i], xy_s.at[i], xy_r.at[i], dev(dx=dx, dy=dy)))
     ag_forward(0)
-    ag_send(3)
     v = g1[me]
     for i, cp in enumerate(cps):
         cp.wait_recv()
@@ -337,7 +335,6 @@
     zb[z] = v
     cps = [rc(zb.at[z], zb.at[z], z_s.at[d - 1], z_r.at[d - 1], dev(dz=d)) for d in range(1, 8)]
     ag_forward(1)
-    ag_send(4)
     for cp in cps:
         cp.wait_recv()
     sends += cps
@@ -350,10 +347,8 @@
     ]
     sends += cps
     ag_forward(2)
+    c_part(0, (0, 1, 2), True)
     ag_forward(3)
-    ag_end(0)
-    ag_end(1)
-    c_work(0)
     for cp in cps:
         cp.wait_recv()
     cp = rc(gf.at[c], gf.at[c], core_s.at[1], core_r.at[1], other)
@@ -382,26 +377,32 @@
     put(3, 2, jnp.where(low, pltpu.roll(v, 64, 1), 0.0))
     put(4, 2, panel(7))
 
-    x_start(0)
+    ag_end(0)
+    ag_end(1)
+    c_part(0, (3,), False)
+    c_send(0)
     ag_end(2)
     ag_end(3)
     c_work(1)
+    x_start(0)
     ag_end(4)
     c_work(2)
     x_start(1)
-    z_start(0)
     chol_step(0, n_ref)
     x_start(2)
+    z_start(0)
     chol_step(1, n_ref)
+    chol_step(2, n_ref)
+    z_start(1)
     z_end(0)
-    z_start(1)
-    chol_step(2, n_ref)
+    chol_step(3, n_ref)
     z_start(2)
-    chol_step(3, n_ref)
+    chol_step(4, n_ref)
+    basis(0, 4)
     z_end(1)
-    chol_step(4, n_ref)
+    basis(4, 7)
     z_end(2)
-    basis()
+    basis(7, 8)
     projected()
     for cp in sends:
         cp.wait_send()

time: 87.7 us -> 95.8 us (1.092)
  Pallas kernels: 84.9 us -> 93 us
    pallas_call x1, Pallas kernels: 84.9 us -> 93 us  [local(): pl.pallas_call(main_kernel, out_shape=(vm((K, 2048), F32), vm((32, K), F3...]
where the time goes in v4:
time: 95.8 us
  Pallas kernels  93 us (97%)
  local copies, waits for them, and re-layouts  2.11 us (2%)
    pallas_call x1, Pallas kernels, local(): pl.pallas_call(main_kernel, out_shape=(vm((K, 2048), F32), vm((32, K), F3...  93 us
    unnamed x2, local copies, waits for them, and re-layouts  2.11 us

profile of v4, /device:TPU:1, one launch (start us, length us, event | category | flops | bytes accessed | tf_op | source)
XLA Modules:
  0.0 95.8 jit_solution(12128847347875205039)
XLA Ops:
  0.6 93.0 %main.1 = (f32[320,2048]{1,0:T(8,128)S(1)}, f32[32,320]{1,0:T(8,128)S(1)}) custom-call(bf16[2048,2048]{1,0:T(8,128)(2,1)} %a_hbm.1, bf16[320,2048]{1,0:T(8,128)(2,1)} %bitcast.3), custom_call_target="tpu_custom_call" | custom-call | tf_op jit(solution)/shard_map/main/pallas_call | solution.py:415
  93.6 1.5 %copy.6 = f32[2048,320]{0,1:T(8,128)} copy(f32[2048,320]{0,1:T(8,128)S(1)} %bitcast.2) | data formatting | bytes 5242880
  95.1 0.6 copy.7
